TPU v7x, 32 devices: a whole 2x2x4 slice. The times are simulated.
32 devices in a mesh: run: 4 (over z), feat: 2 (over core), vox: 4 (over y, x).
Axes of the slice: x: 2, y: 2, z: 4, core: 2. Of those that a mesh axis runs over, the one named last changes fastest.
Arguments:
- stimulus: bfloat16 [4, 512, 256], P('run', None, 'feat')
- responses: bfloat16 [4, 512, 512], P('run', None, 'vox')
- run_lengths: int32 [4], P('run'), may hold values from 1 to 512, 1536 in all
- lag_steps: int32 [4], replicated, may hold values from 0 to 7, as said below
- ridge_grid: float32 [16], replicated, may hold values from 0.05 to 5
- ridge_pick: int32 [4, 2], P('run'), may hold values from 0 to 15
Outputs:
- weights: float32 [4, 2, 1024, 512], P('run', None, 'feat', 'vox')
- fold_errors: float32 [4, 2, 512], P('run', None, 'vox')
Inputs may be any that keep to these rules, and one draw needn't show every extreme that they name: lag_steps[j] is 2 j or 2 j + 1; lag_steps[0] is 0 and the last entry is 7.
All inputs are finite; a program needn't handle non-finite values. No bound on the sum of `run_lengths` on one device may be relied on, other than what follows from the above.
Results may differ from a plain program's by a relative error of at most 0.0003.
Values may be sent and summed in bfloat16 or wider, within the bound.
A program may use at most 128 MiB of HBM per device.

v0:
```python
import jax
import jax.numpy as jnp
from jax import lax
from jax.sharding import PartitionSpec as P


def carried_in(part, axis, combine, identity, reverse):
    count = lax.axis_size(axis)
    place = lax.axis_index(axis)
    ahead = count - 1 - place if reverse else place
    gathered = jax.tree.map(lambda a: lax.all_gather(a, axis), part)
    state = jax.tree.map(lambda a, e: jnp.zeros_like(a) + jnp.asarray(e, a.dtype), part, identity)

    def one(hop, state):
        source = count - 1 - hop if reverse else hop
        return combine(
            state, jax.tree.map(lambda a: lax.dynamic_index_in_dim(a, source, 0, False), gathered)
        )

    return lax.fori_loop(0, ahead, one, state)


def build_features(stim_run, lag_steps, length):
    count_t = stim_run.shape[0]
    steps_t = jnp.arange(count_t, dtype=jnp.int32)
    pieces = []
    for j in range(lag_steps.shape[0]):
        lag = lag_steps[j]
        shifted = jnp.roll(stim_run, lag, axis=0)
        keep = (steps_t >= lag) & (steps_t < length)
        pieces.append(jnp.where(keep[:, None], shifted, jnp.zeros_like(shifted)))
    stacked = jnp.stack(pieces, axis=2)
    return stacked.reshape(count_t, stim_run.shape[1] * lag_steps.shape[0])


def add_terms(first, second):
    return tuple((left + right for left, right in zip(first, second)))


def solve_fold(full_gram, full_cross, count, penalty, feats, masked, length):
    width = full_gram.shape[0]
    eye = jnp.eye(width, dtype=jnp.float32)
    cross_s = full_cross / count
    feats_wide = feats.astype(jnp.float32)
    target_wide = masked.astype(jnp.float32)

    def one_penalty(value):
        system = full_gram / count + value * eye
        lower = jnp.linalg.cholesky(system)
        inner = lax.linalg.triangular_solve(
            lower, cross_s, left_side=True, lower=True, transpose_a=False
        )
        solved = lax.linalg.triangular_solve(
            lower, inner, left_side=True, lower=True, transpose_a=True
        )
        predicted = jnp.dot(feats_wide, solved, precision=lax.Precision.HIGHEST)
        errors = jnp.sum((target_wide - predicted) ** 2, axis=0) / length.astype(jnp.float32)
        return (solved, errors)

    return lax.map(one_penalty, penalty)


def look_up(picks, ridge_grid):
    table_ids = jnp.arange(ridge_grid.shape[0], dtype=jnp.int32)
    hits = picks[:, None] == table_ids[None, :]
    return jnp.sum(
        jnp.where(hits, ridge_grid[None, :], jnp.zeros_like(ridge_grid)[None, :]), axis=1
    )


def local(stimulus, responses, run_lengths, lag_steps, ridge_grid, ridge_pick):
    whole = lax.all_gather(stimulus, "feat", axis=2, tiled=True)
    length = run_lengths[0]
    feats = build_features(whole[0], lag_steps, length)
    count_feat = lax.axis_size("feat")
    count_vox = lax.axis_size("vox")
    width = feats.shape[1]
    half = width // count_feat
    quarter = width // count_vox
    own_rows = lax.dynamic_slice_in_dim(feats, lax.axis_index("feat") * half, half, 1)
    columns = lax.dynamic_slice_in_dim(feats, lax.axis_index("vox") * quarter, quarter, 1)
    steps_t = jnp.arange(feats.shape[0], dtype=jnp.int32)
    masked = jnp.where((steps_t < length)[:, None], responses[0], jnp.zeros_like(responses[0]))
    contract = (((0,), (0,)), ((), ()))
    gram = lax.dot_general(own_rows, columns, contract, preferred_element_type=jnp.float32)
    cross = lax.dot_general(own_rows, masked, contract, preferred_element_type=jnp.float32)
    count = length.astype(jnp.float32).reshape(1)
    zeros = (jnp.zeros_like(gram), jnp.zeros_like(cross), jnp.zeros_like(count))
    before = carried_in((gram, cross, count), "run", add_terms, zeros, False)
    after = carried_in((gram, cross, count), "run", add_terms, zeros, True)
    rest_gram, rest_cross, rest_count = add_terms(before, after)
    wide_rows = lax.all_gather(rest_gram, "vox", axis=1, tiled=True)
    full_gram, full_cross = (
        lax.all_gather(wide_rows, "feat", axis=0, tiled=True),
        lax.all_gather(rest_cross, "feat", axis=0, tiled=True),
    )
    picks = ridge_pick[0]
    solved, errors = solve_fold(
        full_gram, full_cross, rest_count[0], look_up(picks, ridge_grid), feats, masked, length
    )
    kept = lax.dynamic_slice_in_dim(solved, lax.axis_index("feat") * half, half, 1)
    return (kept[None], errors[None])


def solution(mesh):
    return jax.shard_map(
        local,
        mesh=mesh,
        in_specs=(
            P("run", None, "feat"),
            P("run", None, "vox"),
            P("run"),
            P(),
            P(),
            P("run", None),
        ),
        out_specs=(P("run", None, "feat", "vox"), P("run", None, "vox")),
        check_vma=False,
    )
```

profile of v0, /device:TPU:0, one launch (start us, length us, event | category | flops | bytes accessed | tf_op | source)
XLA Modules:
  0.0 881.4 jit_solution(4735311009072833869)
XLA Ops:
  29.7 13.4 %all-reduce.1 = f32[4]{0:T(128)S(1)} all-reduce(f32[4]{0:T(128)S(1)} %dynamic-update-slice.75), channel_id=1, replica_groups=mesh['run'=4,'feat'=2,'vox'=4] {'run'}, use_global_device_ids=true, to_apply=%add.1 | all-reduce | flops 4 | bytes 32
  43.1 14.8 %all-gather.13.cloned.1.call-done = f32[2048,128]{1,0:T(8,128)} async-done(((f32[512,128]{1,0:T(8,128)}), f32[2048,128]{1,0:T(8,128)}) %all-gather.13.cloned.1.call-update) | async-done | bytes 1048592 | tf_op jit(solution)/shard_map/all_gather | solution.py:11
  57.9 47.5 %all-gather.11.cloned.1.call-done = f32[2048,256]{1,0:T(8,128)} async-done(((f32[512,256]{1,0:T(8,128)}), f32[2048,256]{1,0:T(8,128)}) %all-gather.11.cloned.1.call-update) | async-done | bytes 2097168 | tf_op jit(solution)/shard_map/all_gather | solution.py:11
  117.3 34.1 %all-gather.7.cloned.1.call-done = f32[512,1024]{0,1:T(8,128)} async-done(((f32[512,256]{0,1:T(8,128)}), f32[512,1024]{0,1:T(8,128)}) %all-gather.7.cloned.1.call-update) | async-done | bytes 2097168 | tf_op jit(solution)/shard_map/all_gather | solution.py:92
  166.5 706.2 %while.51 = (s32[]{:T(128)}, f32[2,1024,128]{2,1,0:T(8,128)}, f32[2,128]{1,0:T(2,128)S(1)}, f32[]{:T(128)}, f32[1024,1024]{0,1:T(8,128)}, /*index=5*/f32[2]{0:T(...) while((s32[]{:T(128)}, f32[2,1024,128]{2,1,0:T(8,128)}, ...), condition=%wide.region_23.25_spmd.clone, body=%wide.region_5.24_spmd.clone.sunk | while | flops 5452662272 | bytes 122106424 | solution.py:60
  185.5 11.7 %cholesky.1066 = f32[128,128]{1,0:T(8,128)S(1)} custom-call(f32[128,128]{1,0:T(8,128)S(1)} %cholesky.1065), custom_call_target="Cholesky" | custom-call | tf_op jit(solution)/shard_map/while/body/eval_jaxpr/jit(cholesky)/cholesky | solution.py:49
  213.5 12.3 %cholesky.1069 = f32[128,128]{1,0:T(8,128)S(1)} custom-call(f32[128,128]{1,0:T(8,128)S(1)} %cholesky.1068), custom_call_target="Cholesky" | custom-call | tf_op jit(solution)/shard_map/while/body/eval_jaxpr/jit(cholesky)/cholesky | solution.py:49
  241.4 11.7 %cholesky.1071 = f32[128,128]{1,0:T(8,128)S(1)} custom-call(f32[128,128]{1,0:T(8,128)S(1)} %cholesky.1070), custom_call_target="Cholesky" | custom-call | tf_op jit(solution)/shard_map/while/body/eval_jaxpr/jit(cholesky)/cholesky | solution.py:49
  268.4 11.9 %cholesky.1073 = f32[128,128]{1,0:T(8,128)S(1)} custom-call(f32[128,128]{1,0:T(8,128)S(1)} %cholesky.1072), custom_call_target="Cholesky" | custom-call | tf_op jit(solution)/shard_map/while/body/eval_jaxpr/jit(cholesky)/cholesky | solution.py:49
  295.5 11.7 %cholesky.1075 = f32[128,128]{1,0:T(8,128)S(1)} custom-call(f32[128,128]{1,0:T(8,128)S(1)} %cholesky.1074), custom_call_target="Cholesky" | custom-call | tf_op jit(solution)/shard_map/while/body/eval_jaxpr/jit(cholesky)/cholesky | solution.py:49
  322.5 11.7 %cholesky.1077 = f32[128,128]{1,0:T(8,128)S(1)} custom-call(f32[128,128]{1,0:T(8,128)S(1)} %cholesky.1076), custom_call_target="Cholesky" | custom-call | tf_op jit(solution)/shard_map/while/body/eval_jaxpr/jit(cholesky)/cholesky | solution.py:49
  348.9 12.1 %cholesky.1079 = f32[128,128]{1,0:T(8,128)S(1)} custom-call(f32[128,128]{1,0:T(8,128)S(1)} %cholesky.1078), custom_call_target="Cholesky" | custom-call | tf_op jit(solution)/shard_map/while/body/eval_jaxpr/jit(cholesky)/cholesky | solution.py:49
  375.4 11.7 %cholesky.1080 = f32[128,128]{1,0:T(8,128)S(1)} custom-call(f32[128,128]{1,0:T(8,128)S(1)} %convolution_subtract_fusion.48), custom_call_target="Cholesky" | custom-call | tf_op jit(solution)/shard_map/while/body/eval_jaxpr/jit(cholesky)/cholesky | solution.py:49
  393.9 27.4 %while.52 = (s32[]{:T(128)}, f32[1024,1024]{1,0:T(8,128)}, s32[8,2]{0,1:T(2,128)S(1)}, f32[8,128,128]{2,1,0:T(8,128)}, s32[]{:T(128)}) while((s32[]{:T(128)}, f32[1024,1024]{1,0:T(8,128)}, s32[8,2]{0,1:T(2,128)S(1)}, f32[8,128,128]{2,1,0:T(8,128)}, s32[]{:T(128)}) %tuple.173), condition=%wide.while_cond, body=%wide.while_body.sunk | while | flops 2 | bytes 132705 | solution.py:53
  421.3 79.6 %custom-call.148 = f32[8,128,128]{1,2,0:T(8,128)S(1)} custom-call(f32[8,128,128]{2,1,0:T(8,128)} %get-tuple-element.748), custom_call_target="InvertDiagBlocksLowerTriangular" | custom-call | tf_op jit(solution)/shard_map/while/body/eval_jaxpr/triangular_solve | solution.py:53
  538.2 11.7 %cholesky.1066 = f32[128,128]{1,0:T(8,128)S(1)} custom-call(f32[128,128]{1,0:T(8,128)S(1)} %cholesky.1065), custom_call_target="Cholesky" | custom-call | tf_op jit(solution)/shard_map/while/body/eval_jaxpr/jit(cholesky)/cholesky | solution.py:49
  566.2 11.9 %cholesky.1069 = f32[128,128]{1,0:T(8,128)S(1)} custom-call(f32[128,128]{1,0:T(8,128)S(1)} %cholesky.1068), custom_call_target="Cholesky" | custom-call | tf_op jit(solution)/shard_map/while/body/eval_jaxpr/jit(cholesky)/cholesky | solution.py:49
  593.7 11.7 %cholesky.1071 = f32[128,128]{1,0:T(8,128)S(1)} custom-call(f32[128,128]{1,0:T(8,128)S(1)} %cholesky.1070), custom_call_target="Cholesky" | custom-call | tf_op jit(solution)/shard_map/while/body/eval_jaxpr/jit(cholesky)/cholesky | solution.py:49
  620.7 11.9 %cholesky.1073 = f32[128,128]{1,0:T(8,128)S(1)} custom-call(f32[128,128]{1,0:T(8,128)S(1)} %cholesky.1072), custom_call_target="Cholesky" | custom-call | tf_op jit(solution)/shard_map/while/body/eval_jaxpr/jit(cholesky)/cholesky | solution.py:49
  647.8 11.7 %cholesky.1075 = f32[128,128]{1,0:T(8,128)S(1)} custom-call(f32[128,128]{1,0:T(8,128)S(1)} %cholesky.1074), custom_call_target="Cholesky" | custom-call | tf_op jit(solution)/shard_map/while/body/eval_jaxpr/jit(cholesky)/cholesky | solution.py:49
  675.0 11.7 %cholesky.1077 = f32[128,128]{1,0:T(8,128)S(1)} custom-call(f32[128,128]{1,0:T(8,128)S(1)} %cholesky.1076), custom_call_target="Cholesky" | custom-call | tf_op jit(solution)/shard_map/while/body/eval_jaxpr/jit(cholesky)/cholesky | solution.py:49
  701.4 11.9 %cholesky.1079 = f32[128,128]{1,0:T(8,128)S(1)} custom-call(f32[128,128]{1,0:T(8,128)S(1)} %cholesky.1078), custom_call_target="Cholesky" | custom-call | tf_op jit(solution)/shard_map/while/body/eval_jaxpr/jit(cholesky)/cholesky | solution.py:49
  746.2 27.4 %while.52 = (s32[]{:T(128)}, f32[1024,1024]{1,0:T(8,128)}, s32[8,2]{0,1:T(2,128)S(1)}, f32[8,128,128]{2,1,0:T(8,128)}, s32[]{:T(128)}) while((s32[]{:T(128)}, f32[1024,1024]{1,0:T(8,128)}, s32[8,2]{0,1:T(2,128)S(1)}, f32[8,128,128]{2,1,0:T(8,128)}, s32[]{:T(128)}) %tuple.173), condition=%wide.while_cond, body=%wide.while_body.sunk | while | flops 2 | bytes 132705 | solution.py:53
  773.6 79.6 %custom-call.148 = f32[8,128,128]{1,2,0:T(8,128)S(1)} custom-call(f32[8,128,128]{2,1,0:T(8,128)} %get-tuple-element.748), custom_call_target="InvertDiagBlocksLowerTriangular" | custom-call | tf_op jit(solution)/shard_map/while/body/eval_jaxpr/triangular_solve | solution.py:53
  (344 shorter events, 407.3 us)
Async XLA Ops:
  7.2 18.7 %copy-start.5 = (bf16[1,512,128]{2,1,0:T(8,128)(2,1)S(1)}, bf16[1,512,128]{2,1,0:T(8,128)(2,1)}, u32[]{:S(2)}) copy-start(bf16[1,512,128]{2,1,0:T(8,128)(2,1)} %param.15) | copy-start | bytes 393220
  7.2 50.7 %all-gather.13.cloned.1.call-start = ((), (), s32[]{:S(2)}) async-start(), calls=%async_computation.3 | async-start | bytes 1310720 | tf_op jit(solution)/shard_map/all_gather | solution.py:11
  24.5 3.8 copy-start.9
  25.8 79.6 %copy-start.2 = (bf16[512,1024]{0,1:T(8,128)(2,1)}, bf16[512,1024]{0,1:T(8,128)(2,1)S(1)}, u32[]{:S(2)}) copy-start(bf16[512,1024]{0,1:T(8,128)(2,1)S(1)} %reshape.193) | copy-start | bytes 3145732
  27.1 78.3 %all-gather.11.cloned.1.call-start = ((), (), s32[]{:S(2)}) async-start(), calls=%async_computation.2 | async-start | bytes 2621440 | tf_op jit(solution)/shard_map/all_gather | solution.py:11
  28.3 123.2 %all-gather.7.cloned.1.call-start = ((), (), s32[]{:S(2)}) async-start(), calls=%async_computation | async-start | bytes 2621440 | tf_op jit(solution)/shard_map/all_gather | solution.py:92
  116.1 36.9 %copy-start.7 = (f32[16]{0:T(128)S(1)}, f32[16]{0:T(128)}, u32[]{:S(2)}) copy-start(f32[16]{0:T(128)} %param.18) | copy-start | bytes 196
  116.1 36.9 %copy-start.8 = (s32[1,2]{1,0:T(1,128)S(1)}, s32[1,2]{1,0:T(1,128)}, u32[]{:S(2)}) copy-start(s32[1,2]{1,0:T(1,128)} %param.19) | copy-start | bytes 28
  117.2 49.3 %all-gather.9.cloned.1.call-start = ((), (), s32[]{:S(2)}) async-start(), calls=%async_computation.1 | async-start | bytes 6291456 | tf_op jit(solution)/shard_map/all_gather | solution.py:94
  183.5 2.0 copy-start.1
  500.9 8.2 copy-start
  511.8 5.2 copy-start.3
  517.1 2.0 copy-start.4
  536.2 2.0 copy-start.1
  853.2 8.2 copy-start
  864.2 5.2 copy-start.3
  869.4 2.0 copy-start.4
  872.7 1.9 copy-start.6
Sparse Core Ops, SparseCore 0:
  27.2 30.6 all-gather.12
  60.0 45.3 all-gather.10
  117.4 34.0 all-gather.6
  152.8 13.6 all-gather.8
where the time goes:
time: 888 us; the launch traced here: 881 us
  other arithmetic  548 us (62%)
  waiting for transfers between devices  108 us (12%)
  local copies, waits for them, and re-layouts  86 us (10%)
  matrix products  83.5 us (9%)
  between operations  22.6 us (3%)
  blocking collectives  17.9 us (2%)
  loops' own time  15.6 us (2%)
    another operation x60, other arithmetic, one_penalty(): lower = jnp.linalg.cholesky(system)  345 us
    another operation x6, other arithmetic, one_penalty(): lax.linalg.triangular_solve(lower, inner, left_side=True, lower=True, tra...  169 us
    all_gather x2, waiting for transfers between devices, carried_in(): gathered = jax.tree.map(lambda a: lax.all_gather(a, axis), part)  62.3 us
    another operation x48, local copies, waits for them, and re-layouts  54.7 us
    another operation x28, matrix products, one_penalty(): lower = jnp.linalg.cholesky(system)  46.2 us
    all_gather x1, waiting for transfers between devices, local(): wide_rows = lax.all_gather(rest_gram, 'vox', axis=1, tiled=True)  34.1 us
    another operation x30, matrix products, one_penalty(): lax.linalg.triangular_solve(lower, cross_s, left_side=True, lower=True, t...  19.5 us
  transfers between devices with their start and end apart: 4, of which 4 were waited for; matrix products, arithmetic and copies ran while one was open for 0% of the time, Pallas kernels for 0%

commit v1 on v0

v1 whole, which is shorter than its diff:
```python
import functools

import jax
import jax.numpy as jnp
from jax import lax
from jax.experimental import pallas as pl
from jax.experimental.pallas import tpu as pltpu
from jax.sharding import PartitionSpec as P

MESH = pl.DeviceIdType.MESH
B = 128
SUB = 8
F32 = jnp.float32
BF16 = jnp.bfloat16
HI = lax.Precision.HIGHEST


def gather_kernel(runs, stim, resp, length, stim_all, resp_all, len_all, own_sem, s1, r1, s2, r2):
    me = lax.axis_index("run")
    core = lax.axis_index("feat")
    other = 1 - core
    half = resp.shape[0] // 2
    rows = pl.ds(pl.multiple_of(core * half, 16), half)
    barrier = pltpu.get_barrier_semaphore()
    for d in range(1, runs):
        pl.semaphore_signal(
            barrier, inc=1, device_id={"run": lax.rem(me + d, runs)}, device_id_type=MESH
        )
    pl.semaphore_signal(barrier, inc=1, device_id={"feat": other}, device_id_type=MESH)
    pl.semaphore_wait(barrier, runs)

    def to_run(src, dst, which, d):
        return pltpu.make_async_remote_copy(
            src_ref=src,
            dst_ref=dst,
            send_sem=s1.at[which, d - 1],
            recv_sem=r1.at[which, d - 1],
            device_id={"run": lax.rem(me + d, runs)},
            device_id_type=MESH,
        )

    def to_core(src, which, d):
        return pltpu.make_async_remote_copy(
            src_ref=src,
            dst_ref=src,
            send_sem=s2.at[which, d],
            recv_sem=r2.at[which, d],
            device_id={"feat": other},
            device_id_type=MESH,
        )

    first = []
    for d in range(1, runs):
        first.append(
            (
                to_run(stim, stim_all.at[d, core], 0, d),
                to_run(resp.at[rows], resp_all.at[d - 1, rows], 1, d),
                to_run(length, len_all.at[d - 1], 2, d),
            )
        )
    for trio in first:
        for copy in trio:
            copy.start()
    own = pltpu.make_async_copy(stim, stim_all.at[0, core], own_sem)
    own.start()
    own.wait()
    second = [to_core(stim_all.at[0, core], 0, 0)]
    second[0].start()
    for d in range(1, runs):
        first[d - 1][0].wait_recv()
        a = to_core(stim_all.at[d, core], 0, d)
        a.start()
        first[d - 1][1].wait_recv()
        b = to_core(resp_all.at[d - 1, rows], 1, d)
        b.start()
        first[d - 1][2].wait_recv()
        second += [a, b]
    for trio in first:
        for copy in trio:
            copy.wait_send()
    for copy in second:
        copy.wait()


def gather(stim, resp, length, runs):
    time, width = stim.shape
    vox = resp.shape[1]
    anyspace = pl.BlockSpec(memory_space=pl.ANY)
    return pl.pallas_call(
        functools.partial(gather_kernel, runs),
        out_shape=(
            jax.ShapeDtypeStruct((runs, 2, time, width), stim.dtype),
            jax.ShapeDtypeStruct((runs - 1, time, vox), resp.dtype),
            jax.ShapeDtypeStruct((runs - 1, 8, 128), jnp.int32),
        ),
        in_specs=[anyspace] * 3,
        out_specs=(anyspace,) * 3,
        scratch_shapes=[
            pltpu.SemaphoreType.DMA,
            pltpu.SemaphoreType.DMA((3, runs - 1)),
            pltpu.SemaphoreType.DMA((3, runs - 1)),
            pltpu.SemaphoreType.DMA((2, runs)),
            pltpu.SemaphoreType.DMA((2, runs)),
        ],
        compiler_params=pltpu.CompilerParams(collective_id=0, has_side_effects=True),
    )(stim, resp, length)


def invert(block):
    count = B // SUB
    rows = [block[SUB * i : SUB * (i + 1), :] for i in range(count)]
    lane = lax.broadcasted_iota(jnp.int32, (SUB, B), 1)
    sub = lax.broadcasted_iota(jnp.int32, (SUB, B), 0)

    def wide(x):
        return jnp.broadcast_to(x, (SUB, B))

    for s in range(count):
        at = SUB * s
        inside = (lane >= at) & (lane < at + SUB)
        panel = rows[s]
        cols = [wide(panel[:, at + j : at + j + 1]) for j in range(SUB)]
        e = [[wide(cols[j][i : i + 1, :]) for j in range(i + 1)] for i in range(SUB)]
        start = jnp.where(inside, jnp.where(lane == at + sub, 1.0, 0.0), panel)
        r = [wide(start[i : i + 1, :]) for i in range(SUB)]
        scale, low = [], []
        for p in range(SUB):
            q = 1.0 / e[p][p]
            scale.append(q)
            l = {i: e[i][p] * q for i in range(p + 1, SUB)}
            low.append(l)
            for i in range(p + 1, SUB):
                for j in range(p + 1, i + 1):
                    e[i][j] = e[i][j] - l[i] * e[j][p]
            for i in range(p + 1, SUB):
                r[i] = r[i] - l[i] * r[p]
        for p in range(SUB):
            r[p] = r[p] * scale[p]
        for i in range(SUB - 1, 0, -1):
            for p in range(i):
                r[p] = r[p] - low[p][i] * r[i]
        order = [(s + 1 + t) % count for t in range(count - 1)]
        for t in order:
            row = rows[t]
            acc = jnp.where(inside, 0.0, row)
            for p in range(SUB):
                acc = acc - wide(row[:, at + p : at + p + 1]) * r[p]
            rows[t] = acc
        new = r[0]
        for i in range(1, SUB):
            new = jnp.where(sub == i, r[i], new)
        rows[s] = new
    return jnp.concatenate(rows, axis=0)


def solve_kernel(
    lags, grid, pick, stim, resp, lens, own_resp, own_len, w_out, err_out, xs, phi, tgt, m, pinv
):
    others, time, vox = resp.shape
    nlag = lags.shape[0]
    feat = stim.shape[1]
    width = feat * nlag * B
    blocks = width // B
    chunk = others if others <= 4 else 1
    steps = lax.broadcasted_iota(jnp.int32, (time, B), 0)

    def features(run, length, at):
        keep = steps < length
        for f in range(feat):
            xs[pl.ds(8, time), :] = stim[run, f].astype(F32)
            for j in range(nlag):
                moved = xs[pl.ds(8 - lags[j], time), :]
                phi[pl.ds(at, time), pl.ds((f * nlag + j) * B, B)] = jnp.where(
                    keep, moved, 0.0
                ).astype(BF16)

    def products(total, first):
        full = total.shape[0]
        for i in range(0, blocks, 2):
            lhs = total[:, i * B : (i + 2) * B]
            part = lax.dot_general(
                lhs, total[:, i * B :], (((0,), (0,)), ((), ())), preferred_element_type=F32
            )
            if first:
                m[i * B : (i + 2) * B, i * B : width] = part
            else:
                m[i * B : (i + 2) * B, i * B : width] += part
        part = lax.dot_general(
            total, tgt[:full, :], (((0,), (0,)), ((), ())), preferred_element_type=F32
        )
        if first:
            m[:, width:] = part
        else:
            m[:, width:] += part

    xs[pl.ds(0, 8), :] = jnp.zeros((8, B), F32)
    if chunk == others:
        for i in range(others):
            features(i + 1, lens[i, 0:1, :], i * time)
            tgt[pl.ds(i * time, time), :] = resp[i]
        products(phi[...], True)
    else:
        m[...] = jnp.zeros_like(m)

        def one(i, c):
            features(i + 1, lens[i, 0:1, :], 0)
            tgt[...] = resp[i]
            products(phi[...], False)
            return c

        lax.fori_loop(0, others, one, 0)

    count = jnp.sum(lens[:, 0, :], axis=0, keepdims=True).astype(F32)
    ridge = grid[pick[0, lax.axis_index("feat")]] * count
    diag = lax.broadcasted_iota(jnp.int32, (B, B), 0) == lax.broadcasted_iota(
        jnp.int32, (B, B), 1
    )
    shift = jnp.where(diag, ridge, 0.0)

    def step(k, c):
        base = pl.multiple_of(k * B, B)
        pinv[...] = invert(m[pl.ds(base, B), pl.ds(base, B)] + shift)
        for kk in range(blocks):

            @pl.when(k == kk)
            def _():
                lo = (kk + 1) * B
                u = m[kk * B : lo, lo:]
                v = jnp.dot(pinv[...], u, precision=HI, preferred_element_type=F32)
                for i in range(kk + 1, blocks, 2):
                    n = min(2, blocks - i)
                    off = i * B - lo
                    m[i * B : (i + n) * B, i * B :] -= lax.dot_general(
                        u[:, off : off + n * B],
                        v[:, off:],
                        (((0,), (0,)), ((), ())),
                        precision=HI,
                        preferred_element_type=F32,
                    )
                m[kk * B : lo, lo:] = v

        return c

    lax.fori_loop(0, blocks, step, 0)

    for k in range(blocks - 2, -1, -1):
        lo = (k + 1) * B
        m[k * B : lo, width:] -= jnp.dot(
            m[k * B : lo, lo:width], m[lo:, width:], precision=HI, preferred_element_type=F32
        )
    x = m[:, width:]
    for f in range(feat):
        for j in range(nlag):
            w_out[f, pl.ds(j, B, stride=nlag), :] = x[(f * nlag + j) * B : (f * nlag + j + 1) * B]
    top = x.astype(BF16)
    rest = x - top.astype(F32)
    mid = rest.astype(BF16)
    low = (rest - mid.astype(F32)).astype(BF16)
    features(0, own_len[0:1, :], 0)
    made = jnp.dot(
        phi[:time, :], jnp.concatenate([top, mid, low], axis=1), preferred_element_type=F32
    )
    made = made[:, :vox] + (made[:, vox : 2 * vox] + made[:, 2 * vox :])
    target = jnp.where(steps < own_len[0:1, :], own_resp[...].astype(F32), 0.0)
    error = jnp.sum((target - made) ** 2, axis=0, keepdims=True)
    err_out[...] = jnp.broadcast_to(error / own_len[0:1, :].astype(F32), err_out.shape)


def solve(lags, grid, pick, stim, resp, lens, own_resp, own_len):
    others, time, vox = resp.shape
    feat = stim.shape[1]
    width = feat * lags.shape[0] * B
    depth = time * (others if others <= 4 else 1)
    vmem = pl.BlockSpec(memory_space=pltpu.VMEM)
    smem = pl.BlockSpec(memory_space=pltpu.SMEM)
    return pl.pallas_call(
        solve_kernel,
        out_shape=(
            jax.ShapeDtypeStruct((feat, width // feat, vox), F32),
            jax.ShapeDtypeStruct((8, vox), F32),
        ),
        in_specs=[smem] * 3 + [vmem] * 5,
        out_specs=(vmem, vmem),
        scratch_shapes=[
            pltpu.VMEM((time + 8, B), F32),
            pltpu.VMEM((depth, width), BF16),
            pltpu.VMEM((depth, vox), BF16),
            pltpu.VMEM((width, width + vox), F32),
            pltpu.VMEM((B, B), F32),
        ],
        compiler_params=pltpu.CompilerParams(vmem_limit_bytes=56 * 1024 * 1024),
    )(lags, grid, pick, stim, resp, lens, own_resp, own_len)


def swap_kernel(w, err, w_all, err_all, send, recv, local):
    core = lax.axis_index("feat")
    other = 1 - core
    barrier = pltpu.get_barrier_semaphore()
    pl.semaphore_signal(barrier, inc=1, device_id={"feat": other}, device_id_type=MESH)
    pl.semaphore_wait(barrier, 1)
    copies = [
        pltpu.make_async_remote_copy(
            src_ref=src,
            dst_ref=dst,
            send_sem=send.at[i],
            recv_sem=recv.at[i],
            device_id={"feat": other},
            device_id_type=MESH,
        )
        for i, (src, dst) in enumerate(((w.at[other], w_all.at[core]), (err, err_all.at[core])))
    ]
    copies += [
        pltpu.make_async_copy(w.at[core], w_all.at[core], local.at[0]),
        pltpu.make_async_copy(err, err_all.at[core], local.at[1]),
    ]
    for copy in copies:
        copy.start()
    for copy in copies:
        copy.wait()


def swap(w, err):
    anyspace = pl.BlockSpec(memory_space=pl.ANY)
    return pl.pallas_call(
        swap_kernel,
        out_shape=(
            jax.ShapeDtypeStruct(w.shape, F32),
            jax.ShapeDtypeStruct((2,) + err.shape, F32),
        ),
        in_specs=[anyspace] * 2,
        out_specs=(anyspace,) * 2,
        scratch_shapes=[pltpu.SemaphoreType.DMA((2,))] * 3,
        compiler_params=pltpu.CompilerParams(collective_id=1, has_side_effects=True),
    )(w, err)


def local(stimulus, responses, run_lengths, lag_steps, ridge_grid, ridge_pick):
    runs = lax.axis_size("run")
    length = jnp.broadcast_to(run_lengths.reshape(1, 1), (8, 128))
    stim_all, resp_all, len_all = gather(stimulus[0], responses[0], length, runs)
    w, err = solve(
        lag_steps, ridge_grid, ridge_pick, stim_all, resp_all, len_all, responses[0], length
    )
    w_all, err_all = swap(w, err)
    return (w_all[None], err_all[:, 0, :][None])


def solution(mesh):
    return jax.shard_map(
        local,
        mesh=mesh,
        in_specs=(
            P("run", None, "feat"),
            P("run", None, "vox"),
            P("run"),
            P(),
            P(),
            P("run", None),
        ),
        out_specs=(P("run", None, "feat", "vox"), P("run", None, "vox")),
        check_vma=False,
    )
```

time: 888 us -> 93.2 us (0.10)
  other arithmetic: 548 us -> 0 us
  waiting for transfers between devices: 108 us -> 0 us
  Pallas kernels: 0 us -> 86.5 us
  matrix products: 83.5 us -> 0 us
  local copies, waits for them, and re-layouts: 86 us -> 3.72 us
  between operations: 22.6 us -> 1.29 us
  blocking collectives: 17.9 us -> 0 us
  loops' own time: 15.6 us -> 0 us
    another operation x68 -> x0, other arithmetic: 516 us -> none  [the longest x60 345 us: one_penalty(): lower = jnp.linalg.cholesky(system)]
    all_gather x4 -> x0, waiting for transfers between devices: 108 us -> none  [the longest x2 62.3 us: carried_in(): gathered = jax.tree.map(lambda a: lax.all_gather(a, axis), part)]
    pallas_call x0 -> x3, Pallas kernels: none -> 86.5 us  [the longest x1 55.4 us: solve(): pl.pallas_call(solve_kernel, out_shape=(jax.ShapeDtypeStruct((feat, width...]
    another operation x88 -> x0, matrix products: 77.4 us -> none  [the longest x28 46.2 us: one_penalty(): lower = jnp.linalg.cholesky(system)]
    another operation x75 -> x0, local copies, waits for them, and re-layouts: 60.9 us -> none
    add x10 -> x0, other arithmetic: 18.7 us -> none  [the longest x2 11.3 us: one_penalty(): system = full_gram / count + value * eye]
    another operation x5 -> x0, loops' own time: 15.6 us -> none  [the longest x1 13.5 us: solve_fold(): return lax.map(one_penalty, penalty)]
    unnamed x1 -> x0, blocking collectives: 13.4 us -> none
  transfers between devices with their start and end apart: 4 -> 0, of which waited for: 4 -> 0; matrix products, arithmetic and copies ran while one was open for 0% -> 0% of each run, Pallas kernels for 0% -> 0%
where the time goes in v1:
time: 93.2 us; the launch traced here: 91.5 us
  Pallas kernels  86.5 us (93%)
  local copies, waits for them, and re-layouts  3.72 us (4%)
  between operations  1.29 us (1%)
    pallas_call x1, Pallas kernels, solve(): pl.pallas_call(solve_kernel, out_shape=(jax.ShapeDtypeStruct((feat, width...  55.4 us
    pallas_call x1, Pallas kernels, gather(): pl.pallas_call(functools.partial(gather_kernel, runs), out_shape=(jax.Sha...  21.5 us
    pallas_call x1, Pallas kernels, swap(): pl.pallas_call(swap_kernel, out_shape=(jax.ShapeDtypeStruct(w.shape, F32)...  9.57 us
    unnamed x1, local copies, waits for them, and re-layouts  1.87 us

profile of v1, /device:TPU:0, one launch (start us, length us, event | category | flops | bytes accessed | tf_op | source)
XLA Modules:
  0.0 91.5 jit_solution(9903553559165518855)
XLA Ops:
  1.3 0.6 broadcast_in_dim.11.length.own_len
  1.9 21.5 %shard_map.77 = (bf16[4,2,512,128]{3,2,1,0:T(8,128)(2,1)}, bf16[3,512,128]{2,1,0:T(8,128)(2,1)}, s32[3,8,128]{2,1,0:T(8,128)}) custom-call(bf16[512,128]{1,0:T(8,128)(2,1)} %bitcast.9, bf16[512,128]{1,0:T(8,128)(2,1)} %bitcast.6, s32[8,128]{1,0:T(8,128)} %broadcast_in_dim.11.length.own_len), custom_call_target="tpu_custom_call" | custom-call | tf_op jit(solution)/shard_map/pallas_call | solution.py:89
  23.4 55.4 %shard_map.78 = (f32[2,512,128]{2,1,0:T(8,128)}, f32[8,128]{1,0:T(8,128)}) custom-call(s32[4]{0:T(128)} %lags.1, f32[16]{0:T(128)} %grid.1, s32[1,2]{1,0:T(1,128)} %pick.1, bf16[4,2,512,128]{3,2,1,0:T(8,128)(2,1)} %get-tuple-element.9.stim, bf16[3,512,128]{2,1,0:T(8,128)(2,1)} %get-tuple-element.10.resp, s32[3,8,128]{2,1,0:T(8,128)} %get-tuple-element.11.lens, ...), custom_call_target="tpu_custom_call" | custom-call | tf_op jit(solution)/shard_map/pallas_call | solution.py:276
  78.8 9.6 %shard_map.79 = (f32[2,512,128]{2,1,0:T(8,128)}, f32[2,8,128]{2,1,0:T(8,128)}) custom-call(f32[2,512,128]{2,1,0:T(8,128)} %get-tuple-element.12.w, f32[8,128]{1,0:T(8,128)} %get-tuple-element.13.err), custom_call_target="tpu_custom_call" | custom-call | tf_op jit(solution)/shard_map/pallas_call | solution.py:324
  88.4 1.3 %slice.3 = f32[2,1,128]{2,1,0:T(1,128)} slice(f32[2,8,128]{2,1,0:T(8,128)} %get-tuple-element.15), slice={[0:2], [0:1], [0:128]} | slice | bytes 2048 | tf_op jit(solution)/shard_map/slice | solution.py:345
  89.6 1.9 %copy.10 = f32[1,2,512,128]{3,2,1,0:T(8,128)} copy(f32[1,2,512,128]{3,2,1,0:T(8,128)} %bitcast.8) | data formatting | bytes 1048576

commit v2 on v1

--- a/solution.py
+++ b/solution.py
@@ -15,79 +15,96 @@
 HI = lax.Precision.HIGHEST
 
 
-def gather_kernel(runs, stim, resp, length, stim_all, resp_all, len_all, own_sem, s1, r1, s2, r2):
+def gather_kernel(
+    runs, parts, stim, resp, length, stim_all, resp_all, len_all, own_sem, s1, r1, s2, r2, s3, r3
+):
     me = lax.axis_index("run")
+    place = lax.axis_index("vox")
     core = lax.axis_index("feat")
     other = 1 - core
     half = resp.shape[0] // 2
+    piece = stim.shape[0] // parts
     rows = pl.ds(pl.multiple_of(core * half, 16), half)
+    mine = pl.ds(pl.multiple_of(place * piece, 16), piece)
     barrier = pltpu.get_barrier_semaphore()
-    for d in range(1, runs):
-        pl.semaphore_signal(
-            barrier, inc=1, device_id={"run": lax.rem(me + d, runs)}, device_id_type=MESH
-        )
-    pl.semaphore_signal(barrier, inc=1, device_id={"feat": other}, device_id_type=MESH)
-    pl.semaphore_wait(barrier, runs)
-
-    def to_run(src, dst, which, d):
+    peers = [{"run": lax.rem(me + d, runs)} for d in range(1, runs)]
+    peers += [{"vox": lax.rem(place + d, parts)} for d in range(1, parts)]
+    peers += [{"feat": other}]
+    for peer in peers:
+        pl.semaphore_signal(barrier, inc=1, device_id=peer, device_id_type=MESH)
+    own = pltpu.make_async_copy(stim, stim_all.at[0, core], own_sem)
+    own.start()
+    pl.semaphore_wait(barrier, len(peers))
+
+    def remote(src, dst, send, recv, peer):
         return pltpu.make_async_remote_copy(
             src_ref=src,
             dst_ref=dst,
-            send_sem=s1.at[which, d - 1],
-            recv_sem=r1.at[which, d - 1],
-            device_id={"run": lax.rem(me + d, runs)},
+            send_sem=send,
+            recv_sem=recv,
+            device_id=peer,
             device_id_type=MESH,
         )
 
-    def to_core(src, which, d):
-        return pltpu.make_async_remote_copy(
-            src_ref=src,
-            dst_ref=src,
-            send_sem=s2.at[which, d],
-            recv_sem=r2.at[which, d],
-            device_id={"feat": other},
-            device_id_type=MESH,
-        )
-
-    first = []
+    def to_run(src, dst, which, d):
+        peer = {"run": lax.rem(me + d, runs)}
+        return remote(src, dst, s1.at[which, d - 1], r1.at[which, d - 1], peer)
+
+    def to_core(src, dst, which, d):
+        return remote(src, dst, s3.at[which, d], r3.at[which, d], {"feat": other})
+
+    first = [None]
     for d in range(1, runs):
         first.append(
             (
-                to_run(stim, stim_all.at[d, core], 0, d),
+                to_run(stim.at[mine], stim_all.at[d, core, mine], 0, d),
                 to_run(resp.at[rows], resp_all.at[d - 1, rows], 1, d),
                 to_run(length, len_all.at[d - 1], 2, d),
             )
         )
-    for trio in first:
-        for copy in trio:
-            copy.start()
-    own = pltpu.make_async_copy(stim, stim_all.at[0, core], own_sem)
-    own.start()
+    for which in range(3):
+        for d in range(1, runs):
+            first[d][which].start()
+    third = [to_core(stim, stim_all.at[0, core], 0, 0)]
+    third[0].start()
+    second = [[] for _ in range(runs)]
+    for d in range(1, runs):
+        first[d][0].wait_recv()
+        part = stim_all.at[d, core, mine]
+        for v in range(1, parts):
+            peer = {"vox": lax.rem(place + v, parts)}
+            second[d].append(
+                remote(part, part, s2.at[d - 1, v - 1], r2.at[d - 1, v - 1], peer)
+            )
+            second[d][-1].start()
+    for d in range(1, runs):
+        first[d][1].wait_recv()
+        block = resp_all.at[d - 1, rows]
+        third.append(to_core(block, block, 1, d))
+        third[-1].start()
+    for d in range(1, runs):
+        for copy in second[d]:
+            copy.wait_recv()
+        block = stim_all.at[d, core]
+        third.append(to_core(block, block, 0, d))
+        third[-1].start()
+    for d in range(1, runs):
+        first[d][2].wait_recv()
+        for copy in first[d]:
+            copy.wait_send()
+        for copy in second[d]:
+            copy.wait_send()
     own.wait()
-    second = [to_core(stim_all.at[0, core], 0, 0)]
-    second[0].start()
-    for d in range(1, runs):
-        first[d - 1][0].wait_recv()
-        a = to_core(stim_all.at[d, core], 0, d)
-        a.start()
-        first[d - 1][1].wait_recv()
-        b = to_core(resp_all.at[d - 1, rows], 1, d)
-        b.start()
-        first[d - 1][2].wait_recv()
-        second += [a, b]
-    for trio in first:
-        for copy in trio:
-            copy.wait_send()
-    for copy in second:
+    for copy in third:
         copy.wait()
 
 
-def gather(stim, resp, length, runs):
+def gather(stim, resp, length, runs, parts):
     time, width = stim.shape
     vox = resp.shape[1]
     anyspace = pl.BlockSpec(memory_space=pl.ANY)
     return pl.pallas_call(
-        functools.partial(gather_kernel, runs),
+        functools.partial(gather_kernel, runs, parts),
         out_shape=(
             jax.ShapeDtypeStruct((runs, 2, time, width), stim.dtype),
             jax.ShapeDtypeStruct((runs - 1, time, vox), resp.dtype),
@@ -95,13 +112,10 @@
         ),
         in_specs=[anyspace] * 3,
         out_specs=(anyspace,) * 3,
-        scratch_shapes=[
-            pltpu.SemaphoreType.DMA,
-            pltpu.SemaphoreType.DMA((3, runs - 1)),
-            pltpu.SemaphoreType.DMA((3, runs - 1)),
-            pltpu.SemaphoreType.DMA((2, runs)),
-            pltpu.SemaphoreType.DMA((2, runs)),
-        ],
+        scratch_shapes=[pltpu.SemaphoreType.DMA]
+        + [pltpu.SemaphoreType.DMA((3, runs - 1))] * 2
+        + [pltpu.SemaphoreType.DMA((runs - 1, parts - 1))] * 2
+        + [pltpu.SemaphoreType.DMA((2, runs))] * 2,
         compiler_params=pltpu.CompilerParams(collective_id=0, has_side_effects=True),
     )(stim, resp, length)
 
@@ -292,11 +306,13 @@
     )(lags, grid, pick, stim, resp, lens, own_resp, own_len)
 
 
-def swap_kernel(w, err, w_all, err_all, send, recv, local):
+def swap_kernel(w, err, w_all, err_all, held, got, send, recv, local):
     core = lax.axis_index("feat")
     other = 1 - core
     barrier = pltpu.get_barrier_semaphore()
     pl.semaphore_signal(barrier, inc=1, device_id={"feat": other}, device_id_type=MESH)
+    load = pltpu.make_async_copy(w.at[core], held, local.at[0])
+    load.start()
     pl.semaphore_wait(barrier, 1)
     copies = [
         pltpu.make_async_remote_copy(
@@ -307,29 +323,36 @@
             device_id={"feat": other},
             device_id_type=MESH,
         )
-        for i, (src, dst) in enumerate(((w.at[other], w_all.at[core]), (err, err_all.at[core])))
-    ]
-    copies += [
-        pltpu.make_async_copy(w.at[core], w_all.at[core], local.at[0]),
-        pltpu.make_async_copy(err, err_all.at[core], local.at[1]),
+        for i, (src, dst) in enumerate(((w.at[other], w_all.at[core]), (err, got)))
     ]
     for copy in copies:
         copy.start()
-    for copy in copies:
-        copy.wait()
+    load.wait()
+    store = pltpu.make_async_copy(held, w_all.at[core], local.at[1])
+    store.start()
+    copies[1].wait()
+    row = lax.broadcasted_iota(jnp.int32, err_all.shape, 0)
+    err_all[...] = jnp.where(row == core, err[0:2, :], got[0:2, :])
+    copies[0].wait()
+    store.wait()
 
 
 def swap(w, err):
     anyspace = pl.BlockSpec(memory_space=pl.ANY)
+    vmem = pl.BlockSpec(memory_space=pltpu.VMEM)
     return pl.pallas_call(
         swap_kernel,
         out_shape=(
             jax.ShapeDtypeStruct(w.shape, F32),
-            jax.ShapeDtypeStruct((2,) + err.shape, F32),
+            jax.ShapeDtypeStruct((2, err.shape[1]), F32),
         ),
-        in_specs=[anyspace] * 2,
-        out_specs=(anyspace,) * 2,
-        scratch_shapes=[pltpu.SemaphoreType.DMA((2,))] * 3,
+        in_specs=[anyspace, vmem],
+        out_specs=(anyspace, vmem),
+        scratch_shapes=[
+            pltpu.VMEM(w.shape[1:], F32),
+            pltpu.VMEM(err.shape, F32),
+        ]
+        + [pltpu.SemaphoreType.DMA((2,))] * 3,
         compiler_params=pltpu.CompilerParams(collective_id=1, has_side_effects=True),
     )(w, err)
 
@@ -337,12 +360,12 @@
 def local(stimulus, responses, run_lengths, lag_steps, ridge_grid, ridge_pick):
     runs = lax.axis_size("run")
     length = jnp.broadcast_to(run_lengths.reshape(1, 1), (8, 128))
-    stim_all, resp_all, len_all = gather(stimulus[0], responses[0], length, runs)
+    stim_all, resp_all, len_all = gather(stimulus[0], responses[0], length, runs, lax.axis_size("vox"))
     w, err = solve(
         lag_steps, ridge_grid, ridge_pick, stim_all, resp_all, len_all, responses[0], length
     )
     w_all, err_all = swap(w, err)
-    return (w_all[None], err_all[:, 0, :][None])
+    return (w_all[None], err_all[None])
 
 
 def solution(mesh):

time: 93.2 us -> 81.5 us (0.87); the launches traced: 91.5 us -> 81.3 us
  Pallas kernels: 86.5 us -> 76.9 us
    pallas_call x1, Pallas kernels: 9.57 us -> 3.19 us  [swap(): pl.pallas_call(swap_kernel, out_shape=(jax.ShapeDtypeStruct(w.shape, F32)...]
    pallas_call x1, Pallas kernels: 21.5 us -> 18.4 us  [gather(): pl.pallas_call(functools.partial(gather_kernel, runs, parts), out_shape=(...]
    slice x1 -> x0, local copies, waits for them, and re-layouts: 1.26 us -> none  [local(): return (w_all[None], err_all[:, 0, :][None])]
    unnamed x1 -> x4, local copies, waits for them, and re-layouts: 1.87 us -> 2.44 us
where the time goes in v2:
time: 81.5 us; the launch traced here: 81.3 us
  Pallas kernels  76.9 us (94%)
  local copies, waits for them, and re-layouts  3.03 us (4%)
  between operations  1.3 us (2%)
    pallas_call x1, Pallas kernels, solve(): pl.pallas_call(solve_kernel, out_shape=(jax.ShapeDtypeStruct((feat, width...  55.4 us
    pallas_call x1, Pallas kernels, gather(): pl.pallas_call(functools.partial(gather_kernel, runs, parts), out_shape=(...  18.4 us
    pallas_call x1, Pallas kernels, swap(): pl.pallas_call(swap_kernel, out_shape=(jax.ShapeDtypeStruct(w.shape, F32)...  3.19 us
    unnamed x4, local copies, waits for them, and re-layouts  2.44 us

profile of v2, /device:TPU:0, one launch (start us, length us, event | category | flops | bytes accessed | tf_op | source)
XLA Modules:
  0.0 81.3 jit_solution(5285866701769556011)
XLA Ops:
  1.3 0.6 broadcast_in_dim.14.length.own_len
  1.9 18.4 %shard_map.77 = (bf16[4,2,512,128]{3,2,1,0:T(8,128)(2,1)}, bf16[3,512,128]{2,1,0:T(8,128)(2,1)}, s32[3,8,128]{2,1,0:T(8,128)}) custom-call(bf16[512,128]{1,0:T(8,128)(2,1)} %bitcast.9, bf16[512,128]{1,0:T(8,128)(2,1)} %bitcast.6, s32[8,128]{1,0:T(8,128)} %broadcast_in_dim.14.length.own_len), custom_call_target="tpu_custom_call" | custom-call | tf_op jit(solution)/shard_map/pallas_call | solution.py:106
  20.2 55.4 %shard_map.78 = (f32[2,512,128]{2,1,0:T(8,128)}, f32[8,128]{1,0:T(8,128)}) custom-call(s32[4]{0:T(128)} %lags.1, f32[16]{0:T(128)} %grid.1, s32[1,2]{1,0:T(1,128)} %pick.1, bf16[4,2,512,128]{3,2,1,0:T(8,128)(2,1)} %get-tuple-element.9.stim, bf16[3,512,128]{2,1,0:T(8,128)(2,1)} %get-tuple-element.10.resp, s32[3,8,128]{2,1,0:T(8,128)} %get-tuple-element.11.lens, ...), custom_call_target="tpu_custom_call" | custom-call | tf_op jit(solution)/shard_map/pallas_call | solution.py:290
  75.6 3.2 %shard_map.79 = (f32[2,512,128]{2,1,0:T(8,128)}, f32[2,128]{1,0:T(2,128)}) custom-call(f32[2,512,128]{2,1,0:T(8,128)} %get-tuple-element.12.w, f32[8,128]{1,0:T(8,128)} %get-tuple-element.13.err), custom_call_target="tpu_custom_call" | custom-call | tf_op jit(solution)/shard_map/pallas_call | solution.py:343
  78.8 0.0 copy-start
  78.8 1.9 %copy.11 = f32[1,2,512,128]{3,2,1,0:T(8,128)} copy(f32[1,2,512,128]{3,2,1,0:T(8,128)} %bitcast.8) | data formatting | bytes 1048576
  80.7 0.0 copy-done
  80.7 0.6 copy.12
Async XLA Ops:
  78.8 1.9 %copy-start = (f32[2,128]{1,0:T(2,128)S(1)}, f32[2,128]{1,0:T(2,128)}, u32[]{:S(2)}) copy-start(f32[2,128]{1,0:T(2,128)} %get-tuple-element.15) | copy-start | bytes 3076
